TPU v7x, 128 devices: a whole 4x4x4 slice. The times are simulated.
128 devices in a mesh: vir: 4 (over x), occ: 32 (over z, y, core).
Axes of the slice: x: 4, y: 4, z: 4, core: 2. Of those that a mesh axis runs over, the one named last changes fastest.
Arguments:
- amplitudes: bfloat16 [2304, 8, 7168], P(('vir', 'occ')), may hold values from -6 to 6
- integrals: bfloat16 [32, 7168, 1792], P('occ', 'vir'), may hold values from -0.0625 to 0.0625
- nonzero_tile_count: int32 [8], replicated, may hold values from 56 to 112, as said below
- sector_owner: int32 [8], replicated, may hold values from 0 to 7, each once
Outputs:
- residual: bfloat16 [2304, 32, 1792], P('vir', 'occ')
Inputs may be any that keep to these rules, and one draw needn't show every extreme that they name: `nonzero_tile_count`: some sector has all 112 tiles live in every draw. `sector_owner`: each sector appears once.
All inputs are finite; a program needn't handle non-finite values.
Results may differ from a plain program's by a relative error of at most 0.001.
Values may be sent and summed in bfloat16 or wider, within the bound.
A program may use at most 192 MiB of HBM per device.

v0:
```python
import jax
import jax.numpy as jnp
from jax import lax
from jax.sharding import PartitionSpec as P

TILE = 64


def per_device(amplitudes, integrals, nonzero_tile_count, sector_owner):
    sectors = nonzero_tile_count.shape[0]
    sector_group_length = lax.axis_size("occ") // sectors
    occ_index = lax.axis_index("occ")
    pair_width = amplitudes.shape[2]
    column_width = integrals.shape[2]
    block_rows = integrals.shape[1]
    sector_id = sector_owner[occ_index // sector_group_length]
    tile_numbers = jnp.arange(pair_width, dtype=jnp.int32) // TILE
    sector_live = (tile_numbers[None, :] < nonzero_tile_count[:, None]).astype(jnp.bfloat16)
    live_mask = (tile_numbers < nonzero_tile_count[sector_id]).astype(jnp.bfloat16)
    column_mask = lax.dynamic_slice_in_dim(
        live_mask, occ_index % sector_group_length * column_width, column_width
    ).astype(jnp.float32)
    slot_sector = jnp.repeat(sector_owner, sector_group_length)
    slot_live = jnp.take(sector_live, slot_sector, axis=0)
    selected_tiles = jnp.take(amplitudes, slot_sector, axis=1)
    outgoing = selected_tiles * slot_live[None, :, :]
    received = lax.all_to_all(
        lax.all_to_all(outgoing, "vir", split_axis=2, concat_axis=0, tiled=True),
        "occ",
        split_axis=1,
        concat_axis=0,
        tiled=True,
    )
    vir_size = lax.axis_size("vir")
    occ_size = lax.axis_size("occ")
    local_rows = amplitudes.shape[0]
    ordered = received.reshape(occ_size, vir_size, local_rows, block_rows)
    rows_each = occ_size * local_rows
    ladder_product = jnp.einsum(
        "obrc,ca->bora", ordered, integrals[0], preferred_element_type=jnp.float32
    )
    summed = lax.psum_scatter(
        ladder_product.reshape(rows_each * lax.axis_size("vir"), column_width),
        "vir",
        scatter_dimension=0,
        tiled=True,
    )
    return (summed * column_mask[None, :]).astype(jnp.bfloat16)[:, None, :]


def solution(mesh):
    in_specs = (P(("vir", "occ"), None, None), P("occ", "vir", None), P(), P())
    out_specs = P("vir", "occ", None)
    return jax.shard_map(
        per_device, mesh=mesh, in_specs=in_specs, out_specs=out_specs, check_vma=False
    )
```

profile of v0, /device:TPU:1, one launch (start us, length us, event | category | flops | bytes accessed | tf_op | source)
XLA Modules:
  0.0 672.5 jit_solution(8353414315117621252)
XLA Ops:
  6.5 0.9 broadcast_in_dim.30
  7.6 0.6 copy-done.2
  8.2 0.7 compare_convert_fusion
  8.9 0.8 gather_fusion.1
  9.8 23.9 %gather_fusion = bf16[32,18,7168]{2,0,1:T(8,128)(2,1)} fusion(bf16[18,8,7168]{2,1,0:T(8,128)(2,1)S(1)} %copy-done, s32[1024]{0:T(1024)S(1)} %pad_clamp_fusion), kind=kCustom, calls=%fused_computation | custom fusion | bytes 16515200 | tf_op jit(solution)/shard_map/jit(_take)/gather | solution.py:25
  33.8 8.2 %multiply_bitcast_fusion = bf16[18,32,7168]{2,1,0:T(8,128)(2,1)} fusion(bf16[32,18,7168]{2,0,1:T(8,128)(2,1)} %gather_fusion, pred[32]{0:T(512)(128)(4,1)S(1)} %compare_and_fusion, bf16[32,7168]{1,0:T(8,128)(2,1)S(1)} %broadcast_select_fusion), kind=kLoop, calls=%fused_computation.2 | loop fusion | flops 8257536 | bytes 16973856 | tf_op jit(solution)/shard_map/mul | solution.py:26
  42.0 42.1 %copy.16 = bf16[18,32,7168]{1,0,2:T(8,128)(2,1)} copy(bf16[18,32,7168]{2,1,0:T(8,128)(2,1)} %multiply_bitcast_fusion) | data formatting | bytes 16515072 | tf_op jit(solution)/shard_map/mul | solution.py:26
  84.0 47.6 %reshape.94 = bf16[4,2,516096]{2,1,0:T(2,128)(2,1)} reshape(bf16[7168,18,32]{2,1,0:T(8,128)(2,1)} %bitcast.27) | data formatting | bytes 16515072
  131.7 99.6 %all_to_all.33 = bf16[4,2,516096]{2,1,0:T(2,128)(2,1)} all-to-all(bf16[4,2,516096]{2,1,0:T(2,128)(2,1)} %reshape.94), channel_id=1, replica_groups=mesh['vir'=4,'occ'=32] {'vir'}, dimensions={0} | all-to-all | bytes 16515072 | tf_op jit(solution)/shard_map/all_to_all | solution.py:28
  231.3 55.9 %reshape.95 = bf16[7168,18,32]{2,1,0:T(8,128)(2,1)} reshape(bf16[4,2,516096]{2,1,0:T(2,128)(2,1)} %all_to_all.33) | data formatting | bytes 16515072
  287.2 46.3 %copy.23 = bf16[18,32,4,1792]{3,2,1,0:T(4,128)(2,1)} copy(bf16[18,32,4,1792]{1,0,3,2:T(8,128)(2,1)} %bitcast.28) | data formatting | bytes 16515072 | tf_op jit(solution)/shard_map/all_to_all | solution.py:28
  333.5 8.0 %copy.18 = bf16[4,18,32,1792]{3,2,1,0:T(8,128)(2,1)} copy(bf16[4,18,32,1792]{3,0,2,1:T(4,128)(2,1)} %bitcast.29) | data formatting | bytes 16515072 | tf_op jit(solution)/shard_map/all_to_all | solution.py:28
  341.5 11.1 %copy.19 = bf16[72,32,1792]{2,0,1:T(8,128)(2,1)} copy(bf16[72,32,1792]{2,1,0:T(8,128)(2,1)} %bitcast.30) | data formatting | bytes 16515072 | tf_op jit(solution)/shard_map/all_to_all | solution.py:28
  352.6 105.1 %all_to_all.34 = bf16[72,32,1792]{2,0,1:T(8,128)(2,1)} all-to-all(bf16[72,32,1792]{2,0,1:T(8,128)(2,1)} %copy.19), channel_id=1, replica_groups=mesh['vir'=4,'occ'=32] {'occ'}, dimensions={1} | all-to-all | bytes 16515072 | tf_op jit(solution)/shard_map/all_to_all | solution.py:27
  457.7 8.4 %copy.20 = bf16[32,72,1,1792]{3,0,1,2:T(8,128)(2,1)} copy(bf16[32,72,1,1792]{3,1,0,2:T(8,128)(2,1)} %bitcast.31) | data formatting | bytes 16515072 | tf_op jit(solution)/shard_map/all_to_all | solution.py:27
  466.1 19.1 %convolution_bitcast_fusion = f32[4,32,18,1792]{3,1,2,0:T(8,128)S(1)} fusion(bf16[32,4,18,1792]{3,0,2,1:T(8,128)(2,1)} %bitcast.32, bf16[1,1792,1792]{2,1,0:T(8,128)(2,1)} %param.5), kind=kOutput, calls=%fused_computation.3 | convolution fusion | flops 14797504512 | bytes 31195136 | tf_op jit(solution)/shard_map/obrc,ca->bora/dot_general | solution.py:39
  485.3 14.7 %copy.21 = f32[4,32,18,1792]{3,2,1,0:T(8,128)} copy(f32[4,32,18,1792]{3,1,2,0:T(8,128)S(1)} %convolution_bitcast_fusion) | data formatting | bytes 33030144 | tf_op jit(solution)/shard_map/obrc,ca->bora/transpose | solution.py:39
  499.9 18.9 %reshape.76 = f32[2304,1792]{1,0:T(8,128)} reshape(f32[4,32,18,1792]{3,2,1,0:T(8,128)} %copy.21) | data formatting | bytes 33030144 | tf_op jit(solution)/shard_map/reshape | solution.py:43
  518.9 0.8 copy-done.4
  519.6 0.6 dynamic_slice.9
  522.1 0.6 dynamic_slice.10
  522.7 1.4 fusion.6
  524.1 137.3 %reduce-scatter.2.cloned.1.call-done = f32[576,1792]{1,0:T(8,128)} async-done(((f32[2304,1792]{1,0:T(8,128)}), f32[576,1792]{1,0:T(8,128)}) %reduce-scatter.2.cloned.1.call-update) | async-done | bytes 4128784 | tf_op jit(solution)/shard_map/reduce_scatter | solution.py:42
  661.4 3.8 fusion.1
  (17 shorter events, 0.3 us)
Async XLA Ops:
  6.5 3.2 copy-start
  6.5 654.9 %reduce-scatter.2.cloned.1.call-start = ((), (), s32[]{:S(2)}) async-start(), calls=%async_computation.3 | async-start | bytes 20643840 | tf_op jit(solution)/shard_map/reduce_scatter | solution.py:42
  7.6 0.6 copy-start.2
  518.8 146.4 %copy-start.1 = (bf16[18,8,7168]{2,1,0:T(8,128)(2,1)S(1)}, bf16[18,8,7168]{2,1,0:T(8,128)(2,1)}, u32[]{:S(2)}) copy-start(bf16[18,8,7168]{2,1,0:T(8,128)(2,1)} %param.4) | copy-start | bytes 6193156
  518.8 0.8 copy-start.4
  518.8 3.3 copy-start.3
Sparse Core Ops, SparseCore 0:
  519.0 142.3 reduce-scatter.1
where the time goes:
time: 685 us; the launch traced here: 673 us
  local copies, waits for them, and re-layouts  281 us (41%)
  blocking collectives  205 us (30%)
  waiting for transfers between devices  137 us (20%)
  matrix products  19.1 us (3%)
  between operations  15.9 us (2%)
  other arithmetic  14.2 us (2%)
    reduce_scatter x1, waiting for transfers between devices, per_device(): lax.psum_scatter(ladder_product.reshape(rows_each * lax.axis_size('vir'),...  137 us
    all_to_all x1, blocking collectives, per_device(): lax.all_to_all(lax.all_to_all(outgoing, 'vir', split_axis=2, concat_axis=...  105 us
    unnamed x12, local copies, waits for them, and re-layouts  105 us
    all_to_all x1, blocking collectives, per_device(): lax.all_to_all(outgoing, 'vir', split_axis=2, concat_axis=0, tiled=True)  99.6 us
    all_to_all x3, local copies, waits for them, and re-layouts, per_device(): lax.all_to_all(outgoing, 'vir', split_axis=2, concat_axis=0, tiled=True)  65.4 us
    mul x1, local copies, waits for them, and re-layouts, per_device(): outgoing = selected_tiles * slot_live[None, :, :]  42.1 us
    gather x1, local copies, waits for them, and re-layouts, per_device(): selected_tiles = jnp.take(amplitudes, slot_sector, axis=1)  23.9 us
    dot_general x1, matrix products, per_device(): jnp.einsum('obrc,ca->bora', ordered, integrals[0], preferred_element_type...  19.1 us
  transfers between devices with their start and end apart: 1, of which 1 were waited for; matrix products, arithmetic and copies ran while one was open for 0% of the time, Pallas kernels for 0%

commit v1 on v0

v1 whole, which is shorter than its diff:
```python
import functools

import jax
import jax.numpy as jnp
from jax import lax
from jax.experimental import pallas as pl
from jax.experimental.pallas import tpu as pltpu
from jax.sharding import PartitionSpec as P

TILE = 64
MESH = pl.DeviceIdType.MESH
F32, BF16, I16, I32 = jnp.float32, jnp.bfloat16, jnp.int16, jnp.int32

ROWS = 18
SECTORS = 8
PAIR = 2 * ROWS
ZBLOCK = 4 * PAIR
HALF = 896
WIDE = 1792
LANES = 128
BLOCK = ROWS * SECTORS
TOP = 32752.0

CHUNKS = ((2,), (1, 3), (0,))
FIRST = (0, 1, 3)
PADDED = (48, 80, 48)


def kernel(
    count_ref, owner_ref, amp_ref, v_hbm, out_ref,
    raw, send0, send1, send2, got0, got1, got2, v_ref, perm, sel0, sel1, block, prod,
    far_out, far_in, near_out, near_in, far_out_s, far_in_s, near_out_s, near_in_s,
    v_sem, xs, xr, zs, zr, cs, cr, ys, yr, fs, fr, fas, far_, nes, ner, fass, fars, ness, ners,
):
    x = lax.axis_index("vir")
    o = lax.axis_index("occ")
    z, y, c = o // 8, (o // 2) % 4, o % 2
    yp, yl = y // 2, y % 2
    other = 3 - y
    partner = yp * 2 + 1 - yl
    sends = (send0, send1, send2)
    gots = (got0, got1, got2)

    def at(xx, zz, yy, cc):
        return (xx, (zz * 4 + yy) * 2 + cc)

    peers = [at((x + dx) % 4, z, y, (c + dc) % 2) for dx in range(4) for dc in range(2) if dx or dc]
    peers += [at(x, (z + dz) % 4, yy, c) for dz in range(4) for yy in (y, other) if dz or yy is other]
    peers += [at(x, z, partner, c)]
    barrier = pltpu.get_barrier_semaphore()
    for peer in peers:
        pl.semaphore_signal(barrier, inc=1, device_id=peer, device_id_type=MESH)

    v_copy = pltpu.make_async_copy(v_hbm, v_ref, v_sem.at[0])
    v_copy.start()
    pl.semaphore_wait(barrier, len(peers))

    order = (2, 1, 3, 0)

    def x_copy(place, dc):
        to = (x + 4 - order[place]) % 4
        cc = (c + dc) % 2
        src = amp_ref.at[:, pl.ds(pl.multiple_of(to * WIDE + cc * HALF, LANES), HALF)]
        dst = raw.at[pl.ds(pl.multiple_of((place * 2 + c) * BLOCK, 16), BLOCK), :]
        if order[place] == 0 and dc == 0:
            return pltpu.make_async_copy(src, dst, xr.at[place * 2])
        return pltpu.make_async_remote_copy(
            src_ref=src, dst_ref=dst, send_sem=xs.at[place * 2 + dc], recv_sem=xr.at[place * 2 + dc],
            device_id=at(to, z, y, cc), device_id_type=MESH,
        )

    def x_wait(place, dc):
        dst = raw.at[pl.ds(pl.multiple_of((place * 2 + (c + dc) % 2) * BLOCK, 16), BLOCK), :]
        pltpu.make_async_copy(dst, dst, xr.at[place * 2 + dc]).wait()

    for place in range(4):
        for dc in range(2):
            x_copy(place, dc).start()

    row = lax.broadcasted_iota(I32, (LANES, LANES), 0)
    col = lax.broadcasted_iota(I32, (LANES, LANES), 1)
    holds = jnp.zeros((LANES, LANES), I32)
    for g in range(SECTORS):
        holds = jnp.where((row >> 4) == g, owner_ref[g], holds)
    perm[...] = jnp.where(((row & 15) == (col >> 3)) & (holds == (col & 7)), 1.0, 0.0).astype(BF16)

    y_of = (2 * yp, 3 - 2 * yp, 2 * yp + 1, 2 - 2 * yp)
    for sel, padded, parts in ((sel0, PADDED[0], 1), (sel1, PADDED[1], 2)):
        for k in range(parts):
            out_row = lax.broadcasted_iota(I32, (ZBLOCK, 4 * padded), 0)
            in_row = lax.broadcasted_iota(I32, (ZBLOCK, 4 * padded), 1)
            base = jnp.zeros_like(in_row) + (y_of[0] * PAIR)
            inner = in_row - k * PAIR
            for j in range(1, 4):
                later = in_row >= j * padded
                base = jnp.where(later, y_of[j] * PAIR, base)
                inner = jnp.where(later, in_row - (j * padded + k * PAIR), inner)
            hit = (inner >= 0) & (inner < PAIR) & (out_row == base + inner)
            sel[k] = jnp.where(hit, 1.0, 0.0).astype(BF16)

    sector = owner_ref[o // 4]
    live = count_ref[sector] * TILE
    live_row = live - x * WIDE
    live_col = live - (o % 4) * WIDE
    v_copy.wait()

    def mask(i, _):
        rows = pl.ds(pl.multiple_of(i * 64, 64), 64)
        r = lax.broadcasted_iota(I32, (64, WIDE), 0) + i * 64
        k = lax.broadcasted_iota(I32, (64, WIDE), 1)
        m = jnp.where((r < live_row) & (k < live_col), 1.0, 0.0).astype(BF16)
        v_ref[rows, :] = v_ref[rows, :] * m
        return 0

    lax.fori_loop(0, WIDE // 64, mask, 0)

    half = pl.ds(pl.multiple_of(c * HALF, LANES), HALF)
    half_other = pl.ds(pl.multiple_of((1 - c) * HALF, LANES), HALF)

    def slot(ch, zz, yy, cols):
        padded = PADDED[ch]
        return gots[ch].at[pl.ds(pl.multiple_of((zz * 4 + yy) * padded, 16), padded), cols]

    def zy_copy(ch, dz, rp):
        padded = PADDED[ch]
        to_z = (z + dz) % 4
        to_y = other if rp else y
        g = to_z * 2 + to_y // 2
        src = sends[ch].at[pl.ds(pl.multiple_of(g * padded, 16), padded), :]
        dst = slot(ch, z, (to_y % 2) * 2 + rp, half)
        i = ch * 8 + dz * 2 + rp
        if dz == 0 and rp == 0:
            return pltpu.make_async_copy(src, dst, zr.at[i])
        return pltpu.make_async_remote_copy(
            src_ref=src, dst_ref=dst, send_sem=zs.at[i], recv_sem=zr.at[i],
            device_id=at(x, to_z, to_y, c), device_id_type=MESH,
        )

    def landed(ch, dz, rp, mine, cols):
        return slot(ch, (z + 4 - dz) % 4, (yl if mine else 1 - yl) * 2 + rp, cols)

    def wait_for(ref, sem):
        pltpu.make_async_copy(ref, ref, sem).wait()

    def pass_on(ch, dz, rp, kind):
        i = ch * 8 + dz * 2 + rp
        ref = landed(ch, dz, rp, kind != "f", half)
        ss, rr, device = {
            "c": (cs, cr, at(x, z, y, 1 - c)),
            "y": (ys, yr, at(x, z, partner, c)),
            "f": (fs, fr, at(x, z, y, 1 - c)),
        }[kind]
        return pltpu.make_async_remote_copy(
            src_ref=ref, dst_ref=ref, send_sem=ss.at[i], recv_sem=rr.at[i],
            device_id=device, device_id_type=MESH,
        )

    def choose(ch):
        padded = PADDED[ch]
        for k in range(len(CHUNKS[ch])):
            for dc in range(2):
                x_wait(FIRST[ch] + k, dc)
        rows = len(CHUNKS[ch]) * 2 * BLOCK
        start = FIRST[ch] * 2 * BLOCK
        for b in range(padded // 16):
            depth = min(LANES, rows - b * LANES)
            picked = jnp.dot(
                perm[:, :depth], raw[start + b * LANES : start + b * LANES + depth, :],
                preferred_element_type=F32,
            ).astype(BF16)
            for g in range(SECTORS):
                sends[ch][g * padded + 16 * b : g * padded + 16 * b + 16, :] = picked[16 * g : 16 * g + 16, :]
        for dz, rp in PLACES:
            zy_copy(ch, dz, rp).start()

    def spread(ch):
        for dz, rp in PLACES:
            wait_for(landed(ch, dz, rp, True, half), zr.at[ch * 8 + dz * 2 + rp])
            pass_on(ch, dz, rp, "y").start()
            pass_on(ch, dz, rp, "c").start()

    def forward(ch):
        for dz, rp in PLACES:
            wait_for(landed(ch, dz, rp, False, half), yr.at[ch * 8 + dz * 2 + rp])
            pass_on(ch, dz, rp, "f").start()

    def collect(ch):
        for dz, rp in PLACES:
            wait_for(landed(ch, dz, rp, True, half_other), cr.at[ch * 8 + dz * 2 + rp])
            wait_for(landed(ch, dz, rp, False, half_other), fr.at[ch * 8 + dz * 2 + rp])

    def multiply(ch, k, zz):
        padded = PADDED[ch]
        sel = (sel1 if ch == 1 else sel0).at[k]
        rows = pl.ds(pl.multiple_of(zz * 4 * padded, 16), 4 * padded)

        def pick(n, _):
            cols = pl.ds(pl.multiple_of(n * 256, 256), 256)
            block[:, cols] = jnp.dot(sel[...], gots[ch][rows, cols], preferred_element_type=F32).astype(BF16)
            return 0

        lax.fori_loop(0, WIDE // 256, pick, 0)

        def tile(n, _):
            cols = pl.ds(pl.multiple_of(n * 256, 256), 256)
            prod[:, cols] = jnp.dot(block[...], v_ref[:, cols], preferred_element_type=F32)
            return 0

        lax.fori_loop(0, WIDE // 256, tile, 0)

    def encode(codes, scale):
        def biggest(i, m):
            rows = pl.ds(pl.multiple_of(i * 16, 16), 16)
            for j in range(WIDE // LANES):
                m = jnp.maximum(m, jnp.abs(prod[rows, j * LANES : (j + 1) * LANES]))
            return m

        top = lax.fori_loop(0, ZBLOCK // 16, biggest, jnp.full((16, LANES), 1e-30, F32))
        scale[...] = top * (1.0 / TOP)
        inv = TOP / top

        def code(i, _):
            rows = pl.ds(pl.multiple_of(i * 16, 16), 16)
            for j in range(WIDE // LANES):
                cols = slice(j * LANES, (j + 1) * LANES)
                codes[rows, cols] = jnp.round(prod[rows, cols] * inv).astype(I32).astype(I16)
            return 0

        lax.fori_loop(0, ZBLOCK // 16, code, 0)

    def add(codes, scale):
        step = scale[...]

        def body(i, _):
            rows = pl.ds(pl.multiple_of(i * 16, 16), 16)
            for j in range(WIDE // LANES):
                cols = slice(j * LANES, (j + 1) * LANES)
                prod[rows, cols] += codes[rows, cols].astype(I32).astype(F32) * step
            return 0

        lax.fori_loop(0, ZBLOCK // 16, body, 0)

    def far_copies(zz):
        to = (x + 1 + 2 * (zz // 2)) % 4
        make = functools.partial(pltpu.make_async_remote_copy, device_id=at(to, z, y, c), device_id_type=MESH)
        return (
            make(src_ref=far_out.at[zz], dst_ref=far_in.at[zz], send_sem=fas.at[zz], recv_sem=far_.at[zz]),
            make(src_ref=far_out_s.at[zz], dst_ref=far_in_s.at[zz], send_sem=fass.at[zz], recv_sem=fars.at[zz]),
        )

    def near_copies(k, zz):
        to = (x + 1 + 2 * k) % 4
        i = k * 4 + zz
        make = functools.partial(pltpu.make_async_remote_copy, device_id=at(to, z, y, c), device_id_type=MESH)
        return (
            make(src_ref=near_out.at[i], dst_ref=near_in.at[i], send_sem=nes.at[i], recv_sem=ner.at[i]),
            make(src_ref=near_out_s.at[i], dst_ref=near_in_s.at[i], send_sem=ness.at[i], recv_sem=ners.at[i]),
        )

    def far_unit(i, _):
        zz = (i % 2) * 2 + i // 2
        multiply(0, 0, zz)
        encode(far_out.at[zz], far_out_s.at[zz])
        for copy in far_copies(zz):
            copy.start()
        return 0

    def near_unit(i, _):
        k = i % 2
        zz = 2 * (1 - k) + i // 2
        multiply(1, k, zz)
        encode(near_out.at[k * 4 + zz], near_out_s.at[k * 4 + zz])
        for copy in near_copies(k, zz):
            copy.start()
        return 0

    def joint_unit(i, _):
        k = i % 2
        zz = 2 * k + i // 2
        multiply(1, k, zz)
        wait_for(far_in.at[zz], far_.at[zz])
        wait_for(far_in_s.at[zz], fars.at[zz])
        add(far_in.at[zz], far_in_s.at[zz])
        encode(near_out.at[k * 4 + zz], near_out_s.at[k * 4 + zz])
        for copy in near_copies(k, zz):
            copy.start()
        return 0

    def last_unit(i, _):
        zz = (i % 2) * 2 + i // 2
        multiply(2, 0, zz)
        for k in range(2):
            j = k * 4 + zz
            wait_for(near_in.at[j], ner.at[j])
            wait_for(near_in_s.at[j], ners.at[j])
            add(near_in.at[j], near_in_s.at[j])
        rows = pl.ds(pl.multiple_of(zz * ZBLOCK, 16), ZBLOCK)
        out_ref[rows, :] = prod[...].astype(BF16)
        return 0

    choose(0)
    spread(0)
    choose(1)
    forward(0)
    spread(1)
    collect(0)
    lax.fori_loop(0, 4, far_unit, 0)
    choose(2)
    forward(1)
    collect(1)
    lax.fori_loop(0, 4, near_unit, 0)
    spread(2)
    lax.fori_loop(0, 4, joint_unit, 0)
    forward(2)
    collect(2)
    lax.fori_loop(0, 4, last_unit, 0)

    for place in range(4):
        for dc in range(2):
            if order[place] or dc:
                x_copy(place, dc).wait_send()
    for ch in range(3):
        for dz, rp in PLACES:
            if dz or rp:
                zy_copy(ch, dz, rp).wait_send()
            for kind in "cyf":
                pass_on(ch, dz, rp, kind).wait_send()

    def sent(i, _):
        for copy in far_copies(i):
            copy.wait_send()
        for k in range(2):
            for copy in near_copies(k, i):
                copy.wait_send()
        return 0

    lax.fori_loop(0, 4, sent, 0)


PLACES = ((0, 0), (0, 1), (1, 0), (3, 0), (1, 1), (3, 1), (2, 0), (2, 1))


def per_device(amplitudes, integrals, nonzero_tile_count, sector_owner):
    dma = pltpu.SemaphoreType.DMA
    vmem = pltpu.VMEM
    codes = [vmem((n, ZBLOCK, WIDE), I16) for n in (4, 4, 8, 8)]
    scales = [vmem((n, 16, LANES), F32) for n in (4, 4, 8, 8)]
    out = pl.pallas_call(
        kernel,
        out_shape=jax.ShapeDtypeStruct((4 * ZBLOCK, WIDE), BF16),
        in_specs=[
            pl.BlockSpec(memory_space=pltpu.SMEM),
            pl.BlockSpec(memory_space=pltpu.SMEM),
            pl.BlockSpec(memory_space=pl.ANY),
            pl.BlockSpec(memory_space=pl.ANY),
        ],
        out_specs=pl.BlockSpec(memory_space=pltpu.VMEM),
        scratch_shapes=[
            vmem((8 * BLOCK, HALF), BF16),
            *[vmem((SECTORS * p, HALF), BF16) for p in PADDED],
            *[vmem((16 * p, WIDE), BF16) for p in PADDED],
            vmem((WIDE, WIDE), BF16),
            vmem((LANES, LANES), BF16),
            vmem((1, ZBLOCK, 4 * PADDED[0]), BF16),
            vmem((2, ZBLOCK, 4 * PADDED[1]), BF16),
            vmem((ZBLOCK, WIDE), BF16),
            vmem((ZBLOCK, WIDE), F32),
            *codes,
            *scales,
            dma((1,)), dma((8,)), dma((8,)),
            *[dma((24,)) for _ in range(8)],
            dma((4,)), dma((4,)), dma((8,)), dma((8,)),
            dma((4,)), dma((4,)), dma((8,)), dma((8,)),
        ],
        compiler_params=pltpu.CompilerParams(
            collective_id=0, has_side_effects=True, vmem_limit_bytes=56 * 1024 * 1024
        ),
        cost_estimate=pl.CostEstimate(
            flops=2 * 16 * ZBLOCK * WIDE * WIDE, bytes_accessed=20_000_000, transcendentals=0
        ),
    )(
        nonzero_tile_count,
        sector_owner,
        amplitudes.reshape(BLOCK, amplitudes.shape[2]),
        integrals.reshape(WIDE, WIDE),
    )
    return out[:, None, :]


def solution(mesh):
    in_specs = (P(("vir", "occ"), None, None), P("occ", "vir", None), P(), P())
    out_specs = P("vir", "occ", None)
    return jax.shard_map(
        per_device, mesh=mesh, in_specs=in_specs, out_specs=out_specs, check_vma=False
    )
```

time: 685 us -> 134 us (0.20); the launches traced: 673 us -> 134 us
  local copies, waits for them, and re-layouts: 281 us -> 3.02 us
  blocking collectives: 205 us -> 0 us
  waiting for transfers between devices: 137 us -> 0 us
  Pallas kernels: 0 us -> 131 us
  matrix products: 19.1 us -> 0 us
  between operations: 15.9 us -> 0.01 us
  other arithmetic: 14.2 us -> 0 us
    all_to_all x2 -> x0, blocking collectives: 205 us -> none  [the longest x1 105 us: per_device(): lax.all_to_all(lax.all_to_all(outgoing, 'vir', split_axis=2, concat_axis=...]
    reduce_scatter x1 -> x0, waiting for transfers between devices: 137 us -> none  [per_device(): lax.psum_scatter(ladder_product.reshape(rows_each * lax.axis_size('vir'),...]
    pallas_call x0 -> x1, Pallas kernels: none -> 131 us  [per_device(): pl.pallas_call(kernel, out_shape=jax.ShapeDtypeStruct((4 * ZBLOCK, WIDE),...]
    unnamed x12 -> x1, local copies, waits for them, and re-layouts: 105 us -> 3.02 us
    all_to_all x4 -> x0, local copies, waits for them, and re-layouts: 73.9 us -> none  [the longest x3 65.4 us: per_device(): lax.all_to_all(outgoing, 'vir', split_axis=2, concat_axis=0, tiled=True)]
    mul x1 -> x0, local copies, waits for them, and re-layouts: 42.1 us -> none  [per_device(): outgoing = selected_tiles * slot_live[None, :, :]]
    gather x2 -> x0, local copies, waits for them, and re-layouts: 24.7 us -> none  [the longest x1 23.9 us: per_device(): selected_tiles = jnp.take(amplitudes, slot_sector, axis=1)]
    dot_general x1 -> x0, matrix products: 19.1 us -> none  [per_device(): jnp.einsum('obrc,ca->bora', ordered, integrals[0], preferred_element_type...]
  transfers between devices with their start and end apart: 1 -> 0, of which waited for: 1 -> 0; matrix products, arithmetic and copies ran while one was open for 0% -> 0% of each run, Pallas kernels for 0% -> 0%
where the time goes in v1:
time: 134 us
  Pallas kernels  131 us (98%)
  local copies, waits for them, and re-layouts  3.02 us (2%)
    pallas_call x1, Pallas kernels, per_device(): pl.pallas_call(kernel, out_shape=jax.ShapeDtypeStruct((4 * ZBLOCK, WIDE),...  131 us
    unnamed x1, local copies, waits for them, and re-layouts  3.02 us

profile of v1, /device:TPU:1, one launch (start us, length us, event | category | flops | bytes accessed | tf_op | source)
XLA Modules:
  0.0 133.7 jit_solution(17415421000939515483)
XLA Ops:
  0.0 130.7 %shard_map.46 = bf16[576,1792]{1,0:T(8,128)(2,1)} custom-call(s32[8]{0:T(128)} %count_ref.1, s32[8]{0:T(128)} %owner_ref.1, bf16[144,7168]{1,0:T(8,128)(2,1)} %bitcast.5, bf16[1792,1792]{1,0:T(8,128)(2,1)} %bitcast.4), custom_call_target="tpu_custom_call" | custom-call | flops 14797504512 | bytes 20000000 | tf_op jit(solution)/shard_map/pallas_call | solution.py:348
  130.7 3.0 %copy.6 = bf16[576,1,1792]{2,0,1:T(8,128)(2,1)} copy(bf16[576,1,1792]{2,0,1:T(8,128)(2,1)} %bitcast.3) | data formatting | bytes 4128768

commit v2 on v1

--- a/solution.py
+++ b/solution.py
@@ -28,7 +28,7 @@
 
 def kernel(
     count_ref, owner_ref, amp_ref, v_hbm, out_ref,
-    raw, send0, send1, send2, got0, got1, got2, v_ref, perm, sel0, sel1, block, prod,
+    raw, send0, send1, send2, got0, got1, got2, v_ref, perm, wide, prod,
     far_out, far_in, near_out, near_in, far_out_s, far_in_s, near_out_s, near_in_s,
     v_sem, xs, xr, zs, zr, cs, cr, ys, yr, fs, fr, fas, far_, nes, ner, fass, fars, ness, ners,
 ):
@@ -83,20 +83,6 @@
     for g in range(SECTORS):
         holds = jnp.where((row >> 4) == g, owner_ref[g], holds)
     perm[...] = jnp.where(((row & 15) == (col >> 3)) & (holds == (col & 7)), 1.0, 0.0).astype(BF16)
-
-    y_of = (2 * yp, 3 - 2 * yp, 2 * yp + 1, 2 - 2 * yp)
-    for sel, padded, parts in ((sel0, PADDED[0], 1), (sel1, PADDED[1], 2)):
-        for k in range(parts):
-            out_row = lax.broadcasted_iota(I32, (ZBLOCK, 4 * padded), 0)
-            in_row = lax.broadcasted_iota(I32, (ZBLOCK, 4 * padded), 1)
-            base = jnp.zeros_like(in_row) + (y_of[0] * PAIR)
-            inner = in_row - k * PAIR
-            for j in range(1, 4):
-                later = in_row >= j * padded
-                base = jnp.where(later, y_of[j] * PAIR, base)
-                inner = jnp.where(later, in_row - (j * padded + k * PAIR), inner)
-            hit = (inner >= 0) & (inner < PAIR) & (out_row == base + inner)
-            sel[k] = jnp.where(hit, 1.0, 0.0).astype(BF16)
 
     sector = owner_ref[o // 4]
     live = count_ref[sector] * TILE
@@ -173,40 +159,37 @@
         for dz, rp in PLACES:
             zy_copy(ch, dz, rp).start()
 
-    def spread(ch):
-        for dz, rp in PLACES:
+    def spread(ch, dz):
+        for rp in range(2):
             wait_for(landed(ch, dz, rp, True, half), zr.at[ch * 8 + dz * 2 + rp])
             pass_on(ch, dz, rp, "y").start()
             pass_on(ch, dz, rp, "c").start()
 
-    def forward(ch):
-        for dz, rp in PLACES:
+    def forward(ch, dz):
+        for rp in range(2):
             wait_for(landed(ch, dz, rp, False, half), yr.at[ch * 8 + dz * 2 + rp])
             pass_on(ch, dz, rp, "f").start()
 
-    def collect(ch):
-        for dz, rp in PLACES:
+    def collect(ch, dz):
+        for rp in range(2):
             wait_for(landed(ch, dz, rp, True, half_other), cr.at[ch * 8 + dz * 2 + rp])
             wait_for(landed(ch, dz, rp, False, half_other), fr.at[ch * 8 + dz * 2 + rp])
 
-    def multiply(ch, k, zz):
-        padded = PADDED[ch]
-        sel = (sel1 if ch == 1 else sel0).at[k]
-        rows = pl.ds(pl.multiple_of(zz * 4 * padded, 16), 4 * padded)
-
-        def pick(n, _):
-            cols = pl.ds(pl.multiple_of(n * 256, 256), 256)
-            block[:, cols] = jnp.dot(sel[...], gots[ch][rows, cols], preferred_element_type=F32).astype(BF16)
-            return 0
-
-        lax.fori_loop(0, WIDE // 256, pick, 0)
-
-        def tile(n, _):
-            cols = pl.ds(pl.multiple_of(n * 256, 256), 256)
-            prod[:, cols] = jnp.dot(block[...], v_ref[:, cols], preferred_element_type=F32)
-            return 0
-
-        lax.fori_loop(0, WIDE // 256, tile, 0)
+    def multiply(ch, dz):
+        height = 4 * PADDED[ch]
+        rows = pl.ds(pl.multiple_of((z + 4 - dz) % 4 * height, 16), height)
+        wide[:height, :] = jnp.dot(gots[ch][rows, :], v_ref[...], preferred_element_type=F32)
+
+    def compact(ch, k):
+        for side in range(2):
+            for part in range(len(CHUNKS[ch])):
+
+                @pl.when((yp == side) & (k == part))
+                def _():
+                    for j in range(4):
+                        to = Y_OF[side][j] * PAIR
+                        start = j * PADDED[ch] + part * PAIR
+                        prod[to : to + PAIR, :] = wide[start : start + PAIR, :]
 
     def encode(codes, scale):
         def biggest(i, m):
@@ -240,80 +223,87 @@
 
         lax.fori_loop(0, ZBLOCK // 16, body, 0)
 
-    def far_copies(zz):
-        to = (x + 1 + 2 * (zz // 2)) % 4
+    def far_copies(i):
+        to = (x + 1 + 2 * (i % 2)) % 4
         make = functools.partial(pltpu.make_async_remote_copy, device_id=at(to, z, y, c), device_id_type=MESH)
         return (
-            make(src_ref=far_out.at[zz], dst_ref=far_in.at[zz], send_sem=fas.at[zz], recv_sem=far_.at[zz]),
-            make(src_ref=far_out_s.at[zz], dst_ref=far_in_s.at[zz], send_sem=fass.at[zz], recv_sem=fars.at[zz]),
-        )
-
-    def near_copies(k, zz):
+            make(src_ref=far_out.at[i], dst_ref=far_in.at[i], send_sem=fas.at[i], recv_sem=far_.at[i]),
+            make(src_ref=far_out_s.at[i], dst_ref=far_in_s.at[i], send_sem=fass.at[i], recv_sem=fars.at[i]),
+        )
+
+    def near_copies(k, i):
         to = (x + 1 + 2 * k) % 4
-        i = k * 4 + zz
+        j = k * 4 + i
         make = functools.partial(pltpu.make_async_remote_copy, device_id=at(to, z, y, c), device_id_type=MESH)
         return (
-            make(src_ref=near_out.at[i], dst_ref=near_in.at[i], send_sem=nes.at[i], recv_sem=ner.at[i]),
-            make(src_ref=near_out_s.at[i], dst_ref=near_in_s.at[i], send_sem=ness.at[i], recv_sem=ners.at[i]),
-        )
-
-    def far_unit(i, _):
-        zz = (i % 2) * 2 + i // 2
-        multiply(0, 0, zz)
-        encode(far_out.at[zz], far_out_s.at[zz])
-        for copy in far_copies(zz):
+            make(src_ref=near_out.at[j], dst_ref=near_in.at[j], send_sem=nes.at[j], recv_sem=ner.at[j]),
+            make(src_ref=near_out_s.at[j], dst_ref=near_in_s.at[j], send_sem=ness.at[j], recv_sem=ners.at[j]),
+        )
+
+    def far_step(i, _):
+        dz = i + i // 2 - 2 * (i // 3)
+        forward(0, dz)
+        collect(0, dz)
+        multiply(0, dz)
+        compact(0, 0)
+        encode(far_out.at[i], far_out_s.at[i])
+        for copy in far_copies(i):
             copy.start()
-        return 0
-
-    def near_unit(i, _):
-        k = i % 2
-        zz = 2 * (1 - k) + i // 2
-        multiply(1, k, zz)
-        encode(near_out.at[k * 4 + zz], near_out_s.at[k * 4 + zz])
-        for copy in near_copies(k, zz):
+
+        @pl.when(i == 0)
+        def _():
+            choose(1)
+
+        spread(1, dz)
+        return 0
+
+    def near_step(i, _):
+        dz = i + i // 2 - 2 * (i // 3)
+        forward(1, dz)
+        collect(1, dz)
+        multiply(1, dz)
+        joint = i % 2
+        alone = 1 - joint
+        compact(1, alone)
+        encode(near_out.at[alone * 4 + i], near_out_s.at[alone * 4 + i])
+        for copy in near_copies(alone, i):
             copy.start()
-        return 0
-
-    def joint_unit(i, _):
-        k = i % 2
-        zz = 2 * k + i // 2
-        multiply(1, k, zz)
-        wait_for(far_in.at[zz], far_.at[zz])
-        wait_for(far_in_s.at[zz], fars.at[zz])
-        add(far_in.at[zz], far_in_s.at[zz])
-        encode(near_out.at[k * 4 + zz], near_out_s.at[k * 4 + zz])
-        for copy in near_copies(k, zz):
+        compact(1, joint)
+        wait_for(far_in.at[i], far_.at[i])
+        wait_for(far_in_s.at[i], fars.at[i])
+        add(far_in.at[i], far_in_s.at[i])
+        encode(near_out.at[joint * 4 + i], near_out_s.at[joint * 4 + i])
+        for copy in near_copies(joint, i):
             copy.start()
-        return 0
-
-    def last_unit(i, _):
-        zz = (i % 2) * 2 + i // 2
-        multiply(2, 0, zz)
+
+        @pl.when(i == 0)
+        def _():
+            choose(2)
+
+        spread(2, dz)
+        return 0
+
+    def last_step(i, _):
+        dz = i + i // 2 - 2 * (i // 3)
+        forward(2, dz)
+        collect(2, dz)
+        multiply(2, dz)
+        compact(2, 0)
         for k in range(2):
-            j = k * 4 + zz
+            j = k * 4 + i
             wait_for(near_in.at[j], ner.at[j])
             wait_for(near_in_s.at[j], ners.at[j])
             add(near_in.at[j], near_in_s.at[j])
-        rows = pl.ds(pl.multiple_of(zz * ZBLOCK, 16), ZBLOCK)
+        rows = pl.ds(pl.multiple_of((z + 4 - dz) % 4 * ZBLOCK, 16), ZBLOCK)
         out_ref[rows, :] = prod[...].astype(BF16)
         return 0
 
     choose(0)
-    spread(0)
-    choose(1)
-    forward(0)
-    spread(1)
-    collect(0)
-    lax.fori_loop(0, 4, far_unit, 0)
-    choose(2)
-    forward(1)
-    collect(1)
-    lax.fori_loop(0, 4, near_unit, 0)
-    spread(2)
-    lax.fori_loop(0, 4, joint_unit, 0)
-    forward(2)
-    collect(2)
-    lax.fori_loop(0, 4, last_unit, 0)
+    for dz in (0, 1, 3, 2):
+        spread(0, dz)
+    lax.fori_loop(0, 4, far_step, 0)
+    lax.fori_loop(0, 4, near_step, 0)
+    lax.fori_loop(0, 4, last_step, 0)
 
     for place in range(4):
         for dc in range(2):
@@ -337,6 +327,7 @@
     lax.fori_loop(0, 4, sent, 0)
 
 
+Y_OF = ((0, 3, 1, 2), (2, 1, 3, 0))
 PLACES = ((0, 0), (0, 1), (1, 0), (3, 0), (1, 1), (3, 1), (2, 0), (2, 1))
 
 
@@ -361,9 +352,7 @@
             *[vmem((16 * p, WIDE), BF16) for p in PADDED],
             vmem((WIDE, WIDE), BF16),
             vmem((LANES, LANES), BF16),
-            vmem((1, ZBLOCK, 4 * PADDED[0]), BF16),
-            vmem((2, ZBLOCK, 4 * PADDED[1]), BF16),
-            vmem((ZBLOCK, WIDE), BF16),
+            vmem((4 * max(PADDED), WIDE), F32),
             vmem((ZBLOCK, WIDE), F32),
             *codes,
             *scales,

time: 134 us -> 122 us (0.910)
  Pallas kernels: 131 us -> 119 us
    pallas_call x1, Pallas kernels: 131 us -> 119 us  [per_device(): pl.pallas_call(kernel, out_shape=jax.ShapeDtypeStruct((4 * ZBLOCK, WIDE),...]
where the time goes in v2:
time: 122 us
  Pallas kernels  119 us (98%)
  local copies, waits for them, and re-layouts  3.02 us (2%)
    pallas_call x1, Pallas kernels, per_device(): pl.pallas_call(kernel, out_shape=jax.ShapeDtypeStruct((4 * ZBLOCK, WIDE),...  119 us
    unnamed x1, local copies, waits for them, and re-layouts  3.02 us

profile of v2, /device:TPU:1, one launch (start us, length us, event | category | flops | bytes accessed | tf_op | source)
XLA Modules:
  0.0 121.5 jit_solution(4964166165322824086)
XLA Ops:
  0.0 118.5 %shard_map.46 = bf16[576,1792]{1,0:T(8,128)(2,1)} custom-call(s32[8]{0:T(128)} %count_ref.1, s32[8]{0:T(128)} %owner_ref.1, bf16[144,7168]{1,0:T(8,128)(2,1)} %bitcast.5, bf16[1792,1792]{1,0:T(8,128)(2,1)} %bitcast.4), custom_call_target="tpu_custom_call" | custom-call | flops 14797504512 | bytes 20000000 | tf_op jit(solution)/shard_map/pallas_call | solution.py:339
  118.5 3.0 %copy.6 = bf16[576,1,1792]{2,0,1:T(8,128)(2,1)} copy(bf16[576,1,1792]{2,0,1:T(8,128)(2,1)} %bitcast.3) | data formatting | bytes 4128768

commit v3 on v2

--- a/solution.py
+++ b/solution.py
@@ -28,7 +28,7 @@
 
 def kernel(
     count_ref, owner_ref, amp_ref, v_hbm, out_ref,
-    raw, send0, send1, send2, got0, got1, got2, v_ref, perm, wide, prod,
+    raw, send0, send1, send2, got0, got1, got2, v_ref, perm, wide, prod, done, out_sem,
     far_out, far_in, near_out, near_in, far_out_s, far_in_s, near_out_s, near_in_s,
     v_sem, xs, xr, zs, zr, cs, cr, ys, yr, fs, fr, fas, far_, nes, ner, fass, fars, ness, ners,
 ):
@@ -73,9 +73,8 @@
         dst = raw.at[pl.ds(pl.multiple_of((place * 2 + (c + dc) % 2) * BLOCK, 16), BLOCK), :]
         pltpu.make_async_copy(dst, dst, xr.at[place * 2 + dc]).wait()
 
-    for place in range(4):
-        for dc in range(2):
-            x_copy(place, dc).start()
+    for dc in range(2):
+        x_copy(0, dc).start()
 
     row = lax.broadcasted_iota(I32, (LANES, LANES), 0)
     col = lax.broadcasted_iota(I32, (LANES, LANES), 1)
@@ -146,6 +145,10 @@
         for k in range(len(CHUNKS[ch])):
             for dc in range(2):
                 x_wait(FIRST[ch] + k, dc)
+        if ch == 0:
+            for place in (1, 2, 3):
+                for dc in range(2):
+                    x_copy(place, dc).start()
         rows = len(CHUNKS[ch]) * 2 * BLOCK
         start = FIRST[ch] * 2 * BLOCK
         for b in range(padded // 16):
@@ -240,8 +243,16 @@
             make(src_ref=near_out_s.at[j], dst_ref=near_in_s.at[j], send_sem=ness.at[j], recv_sem=ners.at[j]),
         )
 
+    def plane(i):
+        return i + i // 2 - 2 * (i // 3)
+
     def far_step(i, _):
-        dz = i + i // 2 - 2 * (i // 3)
+        dz = plane(i)
+
+        @pl.when(i < 3)
+        def _():
+            spread(0, plane(i + 1))
+
         forward(0, dz)
         collect(0, dz)
         multiply(0, dz)
@@ -250,15 +261,23 @@
         for copy in far_copies(i):
             copy.start()
 
-        @pl.when(i == 0)
+        @pl.when(i == 1)
         def _():
             choose(1)
 
-        spread(1, dz)
+        @pl.when(i >= 2)
+        def _():
+            spread(1, plane(i - 2))
+
         return 0
 
     def near_step(i, _):
-        dz = i + i // 2 - 2 * (i // 3)
+        dz = plane(i)
+
+        @pl.when(i < 2)
+        def _():
+            spread(1, plane(i + 2))
+
         forward(1, dz)
         collect(1, dz)
         multiply(1, dz)
@@ -280,11 +299,23 @@
         def _():
             choose(2)
 
-        spread(2, dz)
+        @pl.when(i >= 1)
+        def _():
+            spread(2, plane(i - 1))
+
         return 0
 
+    def out_copy(i):
+        rows = pl.ds(pl.multiple_of((z + 4 - plane(i)) % 4 * ZBLOCK, 16), ZBLOCK)
+        return pltpu.make_async_copy(done.at[i], out_ref.at[rows, :], out_sem.at[i])
+
     def last_step(i, _):
-        dz = i + i // 2 - 2 * (i // 3)
+        dz = plane(i)
+
+        @pl.when(i == 0)
+        def _():
+            spread(2, plane(3))
+
         forward(2, dz)
         collect(2, dz)
         multiply(2, dz)
@@ -294,13 +325,12 @@
             wait_for(near_in.at[j], ner.at[j])
             wait_for(near_in_s.at[j], ners.at[j])
             add(near_in.at[j], near_in_s.at[j])
-        rows = pl.ds(pl.multiple_of((z + 4 - dz) % 4 * ZBLOCK, 16), ZBLOCK)
-        out_ref[rows, :] = prod[...].astype(BF16)
+        done[i] = prod[...].astype(BF16)
+        out_copy(i).start()
         return 0
 
     choose(0)
-    for dz in (0, 1, 3, 2):
-        spread(0, dz)
+    spread(0, 0)
     lax.fori_loop(0, 4, far_step, 0)
     lax.fori_loop(0, 4, near_step, 0)
     lax.fori_loop(0, 4, last_step, 0)
@@ -322,6 +352,7 @@
         for k in range(2):
             for copy in near_copies(k, i):
                 copy.wait_send()
+        out_copy(i).wait()
         return 0
 
     lax.fori_loop(0, 4, sent, 0)
@@ -342,10 +373,10 @@
         in_specs=[
             pl.BlockSpec(memory_space=pltpu.SMEM),
             pl.BlockSpec(memory_space=pltpu.SMEM),
-            pl.BlockSpec(memory_space=pl.ANY),
-            pl.BlockSpec(memory_space=pl.ANY),
+            pl.BlockSpec(memory_space=pltpu.HBM),
+            pl.BlockSpec(memory_space=pltpu.HBM),
         ],
-        out_specs=pl.BlockSpec(memory_space=pltpu.VMEM),
+        out_specs=pl.BlockSpec(memory_space=pl.ANY),
         scratch_shapes=[
             vmem((8 * BLOCK, HALF), BF16),
             *[vmem((SECTORS * p, HALF), BF16) for p in PADDED],
@@ -354,6 +385,8 @@
             vmem((LANES, LANES), BF16),
             vmem((4 * max(PADDED), WIDE), F32),
             vmem((ZBLOCK, WIDE), F32),
+            vmem((4, ZBLOCK, WIDE), BF16),
+            dma((4,)),
             *codes,
             *scales,
             dma((1,)), dma((8,)), dma((8,)),
@@ -362,7 +395,7 @@
             dma((4,)), dma((4,)), dma((8,)), dma((8,)),
         ],
         compiler_params=pltpu.CompilerParams(
-            collective_id=0, has_side_effects=True, vmem_limit_bytes=56 * 1024 * 1024
+            collective_id=0, has_side_effects=True, vmem_limit_bytes=51 * 1024 * 1024
         ),
         cost_estimate=pl.CostEstimate(
             flops=2 * 16 * ZBLOCK * WIDE * WIDE, bytes_accessed=20_000_000, transcendentals=0

time: 122 us -> 112 us (0.918)
  Pallas kernels: 119 us -> 108 us
    pallas_call x1, Pallas kernels: 119 us -> 108 us  [per_device(): pl.pallas_call(kernel, out_shape=jax.ShapeDtypeStruct((4 * ZBLOCK, WIDE),...]
    unnamed x1 -> x5, local copies, waits for them, and re-layouts: 3.02 us -> 2.62 us
where the time goes in v3:
time: 112 us; the launch traced here: 111 us
  Pallas kernels  108 us (96%)
  local copies, waits for them, and re-layouts  2.62 us (2%)
    pallas_call x1, Pallas kernels, per_device(): pl.pallas_call(kernel, out_shape=jax.ShapeDtypeStruct((4 * ZBLOCK, WIDE),...  108 us
    unnamed x5, local copies, waits for them, and re-layouts  2.62 us

profile of v3, /device:TPU:1, one launch (start us, length us, event | category | flops | bytes accessed | tf_op | source)
XLA Modules:
  0.0 110.6 jit_solution(15021083872812606748)
XLA Ops:
  0.0 0.0 copy-start
  0.0 0.7 copy-done
  0.7 0.0 copy-start.1
  0.7 0.7 copy-done.1
  1.3 107.9 %shard_map.46 = bf16[576,1792]{1,0:T(8,128)(2,1)S(1)} custom-call(s32[8]{0:T(128)S(1)} %copy-done, s32[8]{0:T(128)S(1)} %copy-done.1, bf16[144,7168]{1,0:T(8,128)(2,1)} %bitcast.5, bf16[1792,1792]{1,0:T(8,128)(2,1)} %bitcast.4), custom_call_target="tpu_custom_call" | custom-call | flops 14797504512 | bytes 20000000 | tf_op jit(solution)/shard_map/pallas_call | solution.py:370
  109.3 1.3 %copy.6 = bf16[576,1,1792]{2,0,1:T(8,128)(2,1)} copy(bf16[576,1,1792]{2,0,1:T(8,128)(2,1)S(1)} %bitcast.3) | data formatting | bytes 4128768
Async XLA Ops:
  0.0 0.7 copy-start
  0.7 0.7 copy-start.1

commit v4 on v3

--- a/solution.py
+++ b/solution.py
@@ -27,7 +27,8 @@
 
 
 def kernel(
-    count_ref, owner_ref, amp_ref, v_hbm, out_ref,
+    count_hbm, owner_hbm, amp_ref, v_hbm, out_ref,
+    count_ref, owner_ref, int_sem,
     raw, send0, send1, send2, got0, got1, got2, v_ref, perm, wide, prod, done, out_sem,
     far_out, far_in, near_out, near_in, far_out_s, far_in_s, near_out_s, near_in_s,
     v_sem, xs, xr, zs, zr, cs, cr, ys, yr, fs, fr, fas, far_, nes, ner, fass, fars, ness, ners,
@@ -53,6 +54,10 @@
 
     v_copy = pltpu.make_async_copy(v_hbm, v_ref, v_sem.at[0])
     v_copy.start()
+    count_copy = pltpu.make_async_copy(count_hbm, count_ref, int_sem.at[0])
+    owner_copy = pltpu.make_async_copy(owner_hbm, owner_ref, int_sem.at[1])
+    count_copy.start()
+    owner_copy.start()
     pl.semaphore_wait(barrier, len(peers))
 
     order = (2, 1, 3, 0)
@@ -75,6 +80,9 @@
 
     for dc in range(2):
         x_copy(0, dc).start()
+
+    count_copy.wait()
+    owner_copy.wait()
 
     row = lax.broadcasted_iota(I32, (LANES, LANES), 0)
     col = lax.broadcasted_iota(I32, (LANES, LANES), 1)
@@ -185,16 +193,17 @@
 
     def compact(ch, k):
         for side in range(2):
-            for part in range(len(CHUNKS[ch])):
-
-                @pl.when((yp == side) & (k == part))
-                def _():
-                    for j in range(4):
-                        to = Y_OF[side][j] * PAIR
-                        start = j * PADDED[ch] + part * PAIR
-                        prod[to : to + PAIR, :] = wide[start : start + PAIR, :]
-
-    def encode(codes, scale):
+
+            @pl.when(yp == side)
+            def _():
+                for j in range(4):
+                    to = Y_OF[side][j] * PAIR
+                    start = j * PADDED[ch] + k * PAIR
+                    prod[to : to + PAIR, :] = wide[start : start + PAIR, :]
+
+    def encode(places, scale):
+        tiles = WIDE // LANES // len(places)
+
         def biggest(i, m):
             rows = pl.ds(pl.multiple_of(i * 16, 16), 16)
             for j in range(WIDE // LANES):
@@ -202,41 +211,46 @@
             return m
 
         top = lax.fori_loop(0, ZBLOCK // 16, biggest, jnp.full((16, LANES), 1e-30, F32))
+        top = jnp.maximum(top[:8], top[8:])
         scale[...] = top * (1.0 / TOP)
         inv = TOP / top
+        inv = jnp.concatenate([inv, inv], axis=0)
 
         def code(i, _):
             rows = pl.ds(pl.multiple_of(i * 16, 16), 16)
             for j in range(WIDE // LANES):
-                cols = slice(j * LANES, (j + 1) * LANES)
-                codes[rows, cols] = jnp.round(prod[rows, cols] * inv).astype(I32).astype(I16)
+                value = jnp.round(prod[rows, j * LANES : (j + 1) * LANES] * inv)
+                at_tile = (j % tiles) * LANES
+                places[j // tiles][rows, at_tile : at_tile + LANES] = value.astype(I32).astype(I16)
             return 0
 
         lax.fori_loop(0, ZBLOCK // 16, code, 0)
 
-    def add(codes, scale):
+    def add(codes, scale, first, tiles):
         step = scale[...]
+        step = jnp.concatenate([step, step], axis=0)
 
         def body(i, _):
             rows = pl.ds(pl.multiple_of(i * 16, 16), 16)
-            for j in range(WIDE // LANES):
-                cols = slice(j * LANES, (j + 1) * LANES)
-                prod[rows, cols] += codes[rows, cols].astype(I32).astype(F32) * step
+            for j in range(tiles):
+                value = codes[rows, j * LANES : (j + 1) * LANES].astype(I32).astype(F32) * step
+                prod[rows, (first + j) * LANES : (first + j + 1) * LANES] += value
             return 0
 
         lax.fori_loop(0, ZBLOCK // 16, body, 0)
 
-    def far_copies(i):
-        to = (x + 1 + 2 * (i % 2)) % 4
+    def far_copies(k, i):
+        to = (x + 1 + 2 * k) % 4
+        j = i * 2 + k
         make = functools.partial(pltpu.make_async_remote_copy, device_id=at(to, z, y, c), device_id_type=MESH)
         return (
-            make(src_ref=far_out.at[i], dst_ref=far_in.at[i], send_sem=fas.at[i], recv_sem=far_.at[i]),
-            make(src_ref=far_out_s.at[i], dst_ref=far_in_s.at[i], send_sem=fass.at[i], recv_sem=fars.at[i]),
+            make(src_ref=far_out.at[j], dst_ref=far_in.at[j], send_sem=fas.at[j], recv_sem=far_.at[j]),
+            make(src_ref=far_out_s.at[i], dst_ref=far_in_s.at[j], send_sem=fass.at[j], recv_sem=fars.at[j]),
         )
 
     def near_copies(k, i):
         to = (x + 1 + 2 * k) % 4
-        j = k * 4 + i
+        j = i * 2 + k
         make = functools.partial(pltpu.make_async_remote_copy, device_id=at(to, z, y, c), device_id_type=MESH)
         return (
             make(src_ref=near_out.at[j], dst_ref=near_in.at[j], send_sem=nes.at[j], recv_sem=ner.at[j]),
@@ -257,9 +271,10 @@
         collect(0, dz)
         multiply(0, dz)
         compact(0, 0)
-        encode(far_out.at[i], far_out_s.at[i])
-        for copy in far_copies(i):
-            copy.start()
+        encode((far_out.at[i * 2], far_out.at[i * 2 + 1]), far_out_s.at[i])
+        for k in range(2):
+            for copy in far_copies(k, i):
+                copy.start()
 
         @pl.when(i == 1)
         def _():
@@ -281,19 +296,15 @@
         forward(1, dz)
         collect(1, dz)
         multiply(1, dz)
-        joint = i % 2
-        alone = 1 - joint
-        compact(1, alone)
-        encode(near_out.at[alone * 4 + i], near_out_s.at[alone * 4 + i])
-        for copy in near_copies(alone, i):
-            copy.start()
-        compact(1, joint)
-        wait_for(far_in.at[i], far_.at[i])
-        wait_for(far_in_s.at[i], fars.at[i])
-        add(far_in.at[i], far_in_s.at[i])
-        encode(near_out.at[joint * 4 + i], near_out_s.at[joint * 4 + i])
-        for copy in near_copies(joint, i):
-            copy.start()
+        for k in range(2):
+            j = i * 2 + k
+            compact(1, k)
+            wait_for(far_in.at[j], far_.at[j])
+            wait_for(far_in_s.at[j], fars.at[j])
+            add(far_in.at[j], far_in_s.at[j], k * 7, 7)
+            encode((near_out.at[j],), near_out_s.at[j])
+            for copy in near_copies(k, i):
+                copy.start()
 
         @pl.when(i == 0)
         def _():
@@ -321,10 +332,10 @@
         multiply(2, dz)
         compact(2, 0)
         for k in range(2):
-            j = k * 4 + i
+            j = i * 2 + k
             wait_for(near_in.at[j], ner.at[j])
             wait_for(near_in_s.at[j], ners.at[j])
-            add(near_in.at[j], near_in_s.at[j])
+            add(near_in.at[j], near_in_s.at[j], 0, WIDE // LANES)
         done[i] = prod[...].astype(BF16)
         out_copy(i).start()
         return 0
@@ -347,9 +358,9 @@
                 pass_on(ch, dz, rp, kind).wait_send()
 
     def sent(i, _):
-        for copy in far_copies(i):
-            copy.wait_send()
         for k in range(2):
+            for copy in far_copies(k, i):
+                copy.wait_send()
             for copy in near_copies(k, i):
                 copy.wait_send()
         out_copy(i).wait()
@@ -365,19 +376,22 @@
 def per_device(amplitudes, integrals, nonzero_tile_count, sector_owner):
     dma = pltpu.SemaphoreType.DMA
     vmem = pltpu.VMEM
-    codes = [vmem((n, ZBLOCK, WIDE), I16) for n in (4, 4, 8, 8)]
-    scales = [vmem((n, 16, LANES), F32) for n in (4, 4, 8, 8)]
+    codes = [vmem((8, ZBLOCK, cols), I16) for cols in (HALF, HALF, WIDE, WIDE)]
+    scales = [vmem((n, 8, LANES), F32) for n in (4, 8, 8, 8)]
     out = pl.pallas_call(
         kernel,
         out_shape=jax.ShapeDtypeStruct((4 * ZBLOCK, WIDE), BF16),
         in_specs=[
-            pl.BlockSpec(memory_space=pltpu.SMEM),
-            pl.BlockSpec(memory_space=pltpu.SMEM),
+            pl.BlockSpec(memory_space=pltpu.HBM),
+            pl.BlockSpec(memory_space=pltpu.HBM),
             pl.BlockSpec(memory_space=pltpu.HBM),
             pl.BlockSpec(memory_space=pltpu.HBM),
         ],
         out_specs=pl.BlockSpec(memory_space=pl.ANY),
         scratch_shapes=[
+            pltpu.SMEM((SECTORS,), I32),
+            pltpu.SMEM((SECTORS,), I32),
+            dma((2,)),
             vmem((8 * BLOCK, HALF), BF16),
             *[vmem((SECTORS * p, HALF), BF16) for p in PADDED],
             *[vmem((16 * p, WIDE), BF16) for p in PADDED],
@@ -391,8 +405,7 @@
             *scales,
             dma((1,)), dma((8,)), dma((8,)),
             *[dma((24,)) for _ in range(8)],
-            dma((4,)), dma((4,)), dma((8,)), dma((8,)),
-            dma((4,)), dma((4,)), dma((8,)), dma((8,)),
+            *[dma((8,)) for _ in range(8)],
         ],
         compiler_params=pltpu.CompilerParams(
             collective_id=0, has_side_effects=True, vmem_limit_bytes=51 * 1024 * 1024
@@ -401,8 +414,8 @@
             flops=2 * 16 * ZBLOCK * WIDE * WIDE, bytes_accessed=20_000_000, transcendentals=0
         ),
     )(
-        nonzero_tile_count,
-        sector_owner,
+        pltpu.with_memory_space_constraint(nonzero_tile_count, pltpu.HBM),
+        pltpu.with_memory_space_constraint(sector_owner, pltpu.HBM),
         amplitudes.reshape(BLOCK, amplitudes.shape[2]),
         integrals.reshape(WIDE, WIDE),
     )

time: 112 us -> 107 us (0.955); the launches traced: 111 us -> 107 us
  Pallas kernels: 108 us -> 105 us
  local copies, waits for them, and re-layouts: 2.62 us -> 1.31 us
    pallas_call x1, Pallas kernels: 108 us -> 105 us  [per_device(): pl.pallas_call(kernel, out_shape=jax.ShapeDtypeStruct((4 * ZBLOCK, WIDE),...]
    unnamed x5 -> x1, local copies, waits for them, and re-layouts: 2.62 us -> 1.31 us
where the time goes in v4:
time: 107 us
  Pallas kernels  105 us (98%)
  local copies, waits for them, and re-layouts  1.31 us (1%)
    pallas_call x1, Pallas kernels, per_device(): pl.pallas_call(kernel, out_shape=jax.ShapeDtypeStruct((4 * ZBLOCK, WIDE),...  105 us

profile of v4, /device:TPU:1, one launch (start us, length us, event | category | flops | bytes accessed | tf_op | source)
XLA Modules:
  0.0 106.7 jit_solution(9171173828606680170)
XLA Ops:
  0.0 105.4 %shard_map.46 = bf16[576,1792]{1,0:T(8,128)(2,1)S(1)} custom-call(s32[8]{0:T(128)} %count_hbm.1, s32[8]{0:T(128)} %owner_hbm.1, bf16[144,7168]{1,0:T(8,128)(2,1)} %bitcast.5, bf16[1792,1792]{1,0:T(8,128)(2,1)} %bitcast.4), custom_call_target="tpu_custom_call" | custom-call | flops 14797504512 | bytes 20000000 | tf_op jit(solution)/shard_map/pallas_call | solution.py:381
  105.4 1.3 %copy.6 = bf16[576,1,1792]{2,0,1:T(8,128)(2,1)} copy(bf16[576,1,1792]{2,0,1:T(8,128)(2,1)S(1)} %bitcast.3) | data formatting | bytes 4128768

commit v5 on v4

--- a/solution.py
+++ b/solution.py
@@ -31,7 +31,7 @@
     count_ref, owner_ref, int_sem,
     raw, send0, send1, send2, got0, got1, got2, v_ref, perm, wide, prod, done, out_sem,
     far_out, far_in, near_out, near_in, far_out_s, far_in_s, near_out_s, near_in_s,
-    v_sem, xs, xr, zs, zr, cs, cr, ys, yr, fs, fr, fas, far_, nes, ner, fass, fars, ness, ners,
+    v_sem, xs, xr, zs, cs, ys, fs, zr, yr, core_r, fas, far_, nes, ner, fass, fars, ness, ners,
 ):
     x = lax.axis_index("vir")
     o = lax.axis_index("occ")
@@ -70,7 +70,7 @@
         if order[place] == 0 and dc == 0:
             return pltpu.make_async_copy(src, dst, xr.at[place * 2])
         return pltpu.make_async_remote_copy(
-            src_ref=src, dst_ref=dst, send_sem=xs.at[place * 2 + dc], recv_sem=xr.at[place * 2 + dc],
+            src_ref=src, dst_ref=dst, send_sem=xs.at[0], recv_sem=xr.at[place * 2 + dc],
             device_id=at(to, z, y, cc), device_id_type=MESH,
         )
 
@@ -125,7 +125,7 @@
         if dz == 0 and rp == 0:
             return pltpu.make_async_copy(src, dst, zr.at[i])
         return pltpu.make_async_remote_copy(
-            src_ref=src, dst_ref=dst, send_sem=zs.at[i], recv_sem=zr.at[i],
+            src_ref=src, dst_ref=dst, send_sem=zs.at[ch], recv_sem=zr.at[i],
             device_id=at(x, to_z, to_y, c), device_id_type=MESH,
         )
 
@@ -139,12 +139,12 @@
         i = ch * 8 + dz * 2 + rp
         ref = landed(ch, dz, rp, kind != "f", half)
         ss, rr, device = {
-            "c": (cs, cr, at(x, z, y, 1 - c)),
-            "y": (ys, yr, at(x, z, partner, c)),
-            "f": (fs, fr, at(x, z, y, 1 - c)),
+            "c": (cs, core_r.at[ch * 4 + dz], at(x, z, y, 1 - c)),
+            "y": (ys, yr.at[i], at(x, z, partner, c)),
+            "f": (fs, core_r.at[ch * 4 + dz], at(x, z, y, 1 - c)),
         }[kind]
         return pltpu.make_async_remote_copy(
-            src_ref=ref, dst_ref=ref, send_sem=ss.at[i], recv_sem=rr.at[i],
+            src_ref=ref, dst_ref=ref, send_sem=ss.at[ch], recv_sem=rr,
             device_id=device, device_id_type=MESH,
         )
 
@@ -182,9 +182,9 @@
             pass_on(ch, dz, rp, "f").start()
 
     def collect(ch, dz):
-        for rp in range(2):
-            wait_for(landed(ch, dz, rp, True, half_other), cr.at[ch * 8 + dz * 2 + rp])
-            wait_for(landed(ch, dz, rp, False, half_other), fr.at[ch * 8 + dz * 2 + rp])
+        height = 4 * PADDED[ch]
+        rows = pl.ds(pl.multiple_of((z + 4 - dz) % 4 * height, 16), height)
+        wait_for(gots[ch].at[rows, half_other], core_r.at[ch * 4 + dz])
 
     def multiply(ch, dz):
         height = 4 * PADDED[ch]
@@ -244,8 +244,8 @@
         j = i * 2 + k
         make = functools.partial(pltpu.make_async_remote_copy, device_id=at(to, z, y, c), device_id_type=MESH)
         return (
-            make(src_ref=far_out.at[j], dst_ref=far_in.at[j], send_sem=fas.at[j], recv_sem=far_.at[j]),
-            make(src_ref=far_out_s.at[i], dst_ref=far_in_s.at[j], send_sem=fass.at[j], recv_sem=fars.at[j]),
+            make(src_ref=far_out.at[j], dst_ref=far_in.at[j], send_sem=fas.at[0], recv_sem=far_.at[j]),
+            make(src_ref=far_out_s.at[i], dst_ref=far_in_s.at[j], send_sem=fass.at[0], recv_sem=fars.at[j]),
         )
 
     def near_copies(k, i):
@@ -253,8 +253,8 @@
         j = i * 2 + k
         make = functools.partial(pltpu.make_async_remote_copy, device_id=at(to, z, y, c), device_id_type=MESH)
         return (
-            make(src_ref=near_out.at[j], dst_ref=near_in.at[j], send_sem=nes.at[j], recv_sem=ner.at[j]),
-            make(src_ref=near_out_s.at[j], dst_ref=near_in_s.at[j], send_sem=ness.at[j], recv_sem=ners.at[j]),
+            make(src_ref=near_out.at[j], dst_ref=near_in.at[j], send_sem=nes.at[0], recv_sem=ner.at[j]),
+            make(src_ref=near_out_s.at[j], dst_ref=near_in_s.at[j], send_sem=ness.at[0], recv_sem=ners.at[j]),
         )
 
     def plane(i):
@@ -318,7 +318,7 @@
 
     def out_copy(i):
         rows = pl.ds(pl.multiple_of((z + 4 - plane(i)) % 4 * ZBLOCK, 16), ZBLOCK)
-        return pltpu.make_async_copy(done.at[i], out_ref.at[rows, :], out_sem.at[i])
+        return pltpu.make_async_copy(done.at[i], out_ref.at[rows, :], out_sem.at[0])
 
     def last_step(i, _):
         dz = plane(i)
@@ -346,27 +346,16 @@
     lax.fori_loop(0, 4, near_step, 0)
     lax.fori_loop(0, 4, last_step, 0)
 
-    for place in range(4):
-        for dc in range(2):
-            if order[place] or dc:
-                x_copy(place, dc).wait_send()
+    wait_for(raw.at[: 7 * BLOCK, :], xs.at[0])
     for ch in range(3):
-        for dz, rp in PLACES:
-            if dz or rp:
-                zy_copy(ch, dz, rp).wait_send()
-            for kind in "cyf":
-                pass_on(ch, dz, rp, kind).wait_send()
-
-    def sent(i, _):
-        for k in range(2):
-            for copy in far_copies(k, i):
-                copy.wait_send()
-            for copy in near_copies(k, i):
-                copy.wait_send()
-        out_copy(i).wait()
-        return 0
-
-    lax.fori_loop(0, 4, sent, 0)
+        wait_for(sends[ch].at[: 7 * PADDED[ch], :], zs.at[ch])
+        for sem in (cs, ys, fs):
+            wait_for(sends[ch], sem.at[ch])
+    wait_for(far_out, fas.at[0])
+    wait_for(near_out, nes.at[0])
+    wait_for(near_out_s, fass.at[0])
+    wait_for(near_out_s, ness.at[0])
+    wait_for(done, out_sem.at[0])
 
 
 Y_OF = ((0, 3, 1, 2), (2, 1, 3, 0))
@@ -400,12 +389,11 @@
             vmem((4 * max(PADDED), WIDE), F32),
             vmem((ZBLOCK, WIDE), F32),
             vmem((4, ZBLOCK, WIDE), BF16),
-            dma((4,)),
+            dma((1,)),
             *codes,
             *scales,
-            dma((1,)), dma((8,)), dma((8,)),
-            *[dma((24,)) for _ in range(8)],
-            *[dma((8,)) for _ in range(8)],
+            *[dma((n,)) for n in (1, 1, 8, 3, 3, 3, 3, 24, 24, 12)],
+            *[dma((n,)) for n in (1, 8) * 4],
         ],
         compiler_params=pltpu.CompilerParams(
             collective_id=0, has_side_effects=True, vmem_limit_bytes=51 * 1024 * 1024

time: 107 us -> 105 us (0.981)
    pallas_call x1, Pallas kernels: 105 us -> 104 us  [per_device(): pl.pallas_call(kernel, out_shape=jax.ShapeDtypeStruct((4 * ZBLOCK, WIDE),...]
where the time goes in v5:
time: 105 us
  Pallas kernels  104 us (99%)
  local copies, waits for them, and re-layouts  1.31 us (1%)
    pallas_call x1, Pallas kernels, per_device(): pl.pallas_call(kernel, out_shape=jax.ShapeDtypeStruct((4 * ZBLOCK, WIDE),...  104 us

profile of v5, /device:TPU:1, one launch (start us, length us, event | category | flops | bytes accessed | tf_op | source)
XLA Modules:
  0.0 105.1 jit_solution(8852652881566208499)
XLA Ops:
  0.0 103.8 %shard_map.46 = bf16[576,1792]{1,0:T(8,128)(2,1)S(1)} custom-call(s32[8]{0:T(128)} %count_hbm.1, s32[8]{0:T(128)} %owner_hbm.1, bf16[144,7168]{1,0:T(8,128)(2,1)} %bitcast.5, bf16[1792,1792]{1,0:T(8,128)(2,1)} %bitcast.4), custom_call_target="tpu_custom_call" | custom-call | flops 14797504512 | bytes 20000000 | tf_op jit(solution)/shard_map/pallas_call | solution.py:370
  103.8 1.3 %copy.6 = bf16[576,1,1792]{2,0,1:T(8,128)(2,1)} copy(bf16[576,1,1792]{2,0,1:T(8,128)(2,1)S(1)} %bitcast.3) | data formatting | bytes 4128768

commit v6 on v5

--- a/solution.py
+++ b/solution.py
@@ -211,10 +211,10 @@
             return m
 
         top = lax.fori_loop(0, ZBLOCK // 16, biggest, jnp.full((16, LANES), 1e-30, F32))
-        top = jnp.maximum(top[:8], top[8:])
+        top = jnp.max(top, axis=0, keepdims=True)
         scale[...] = top * (1.0 / TOP)
         inv = TOP / top
-        inv = jnp.concatenate([inv, inv], axis=0)
+        inv = jnp.broadcast_to(inv, (16, LANES))
 
         def code(i, _):
             rows = pl.ds(pl.multiple_of(i * 16, 16), 16)
@@ -227,8 +227,7 @@
         lax.fori_loop(0, ZBLOCK // 16, code, 0)
 
     def add(codes, scale, first, tiles):
-        step = scale[...]
-        step = jnp.concatenate([step, step], axis=0)
+        step = jnp.broadcast_to(scale[...], (16, LANES))
 
         def body(i, _):
             rows = pl.ds(pl.multiple_of(i * 16, 16), 16)
@@ -320,6 +319,22 @@
         rows = pl.ds(pl.multiple_of((z + 4 - plane(i)) % 4 * ZBLOCK, 16), ZBLOCK)
         return pltpu.make_async_copy(done.at[i], out_ref.at[rows, :], out_sem.at[0])
 
+    def finish(i):
+        left, right = i * 2, i * 2 + 1
+        steps = [jnp.broadcast_to(near_in_s[j], (16, LANES)) for j in (left, right)]
+
+        def body(n, _):
+            rows = pl.ds(pl.multiple_of(n * 16, 16), 16)
+            for j in range(WIDE // LANES):
+                cols = slice(j * LANES, (j + 1) * LANES)
+                total = prod[rows, cols]
+                for m, step in zip((left, right), steps):
+                    total += near_in[m, rows, cols].astype(I32).astype(F32) * step
+                done[i, rows, cols] = total.astype(BF16)
+            return 0
+
+        lax.fori_loop(0, ZBLOCK // 16, body, 0)
+
     def last_step(i, _):
         dz = plane(i)
 
@@ -335,8 +350,7 @@
             j = i * 2 + k
             wait_for(near_in.at[j], ner.at[j])
             wait_for(near_in_s.at[j], ners.at[j])
-            add(near_in.at[j], near_in_s.at[j], 0, WIDE // LANES)
-        done[i] = prod[...].astype(BF16)
+        finish(i)
         out_copy(i).start()
         return 0
 
@@ -366,7 +380,7 @@
     dma = pltpu.SemaphoreType.DMA
     vmem = pltpu.VMEM
     codes = [vmem((8, ZBLOCK, cols), I16) for cols in (HALF, HALF, WIDE, WIDE)]
-    scales = [vmem((n, 8, LANES), F32) for n in (4, 8, 8, 8)]
+    scales = [vmem((n, 1, LANES), F32) for n in (4, 8, 8, 8)]
     out = pl.pallas_call(
         kernel,
         out_shape=jax.ShapeDtypeStruct((4 * ZBLOCK, WIDE), BF16),

time: 105 us -> 105 us (level)
  no operation moved by 1% of the time
where the time goes in v6:
time: 105 us; the launch traced here: 104 us
  Pallas kernels  103 us (98%)
  local copies, waits for them, and re-layouts  1.31 us (1%)
    pallas_call x1, Pallas kernels, per_device(): pl.pallas_call(kernel, out_shape=jax.ShapeDtypeStruct((4 * ZBLOCK, WIDE),...  103 us

profile of v6, /device:TPU:1, one launch (start us, length us, event | category | flops | bytes accessed | tf_op | source)
XLA Modules:
  0.0 104.4 jit_solution(15701923527430736016)
XLA Ops:
  0.0 103.1 %shard_map.46 = bf16[576,1792]{1,0:T(8,128)(2,1)S(1)} custom-call(s32[8]{0:T(128)} %count_hbm.1, s32[8]{0:T(128)} %owner_hbm.1, bf16[144,7168]{1,0:T(8,128)(2,1)} %bitcast.5, bf16[1792,1792]{1,0:T(8,128)(2,1)} %bitcast.4), custom_call_target="tpu_custom_call" | custom-call | flops 14797504512 | bytes 20000000 | tf_op jit(solution)/shard_map/pallas_call | solution.py:384
  103.1 1.3 %copy.6 = bf16[576,1,1792]{2,0,1:T(8,128)(2,1)} copy(bf16[576,1,1792]{2,0,1:T(8,128)(2,1)S(1)} %bitcast.3) | data formatting | bytes 4128768

commit v7 on v6

--- a/solution.py
+++ b/solution.py
@@ -148,13 +148,18 @@
             device_id=device, device_id_type=MESH,
         )
 
+    def spread_one(ch, dz, rp):
+        wait_for(landed(ch, dz, rp, True, half), zr.at[ch * 8 + dz * 2 + rp])
+        pass_on(ch, dz, rp, "y").start()
+        pass_on(ch, dz, rp, "c").start()
+
     def choose(ch):
         padded = PADDED[ch]
         for k in range(len(CHUNKS[ch])):
             for dc in range(2):
                 x_wait(FIRST[ch] + k, dc)
         if ch == 0:
-            for place in (1, 2, 3):
+            for place in (1, 2):
                 for dc in range(2):
                     x_copy(place, dc).start()
         rows = len(CHUNKS[ch]) * 2 * BLOCK
@@ -169,6 +174,8 @@
                 sends[ch][g * padded + 16 * b : g * padded + 16 * b + 16, :] = picked[16 * g : 16 * g + 16, :]
         for dz, rp in PLACES:
             zy_copy(ch, dz, rp).start()
+        if ch == 0:
+            spread_one(0, 0, 0)
 
     def spread(ch, dz):
         for rp in range(2):
@@ -355,7 +362,9 @@
         return 0
 
     choose(0)
-    spread(0, 0)
+    spread_one(0, 0, 1)
+    for dc in range(2):
+        x_copy(3, dc).start()
     lax.fori_loop(0, 4, far_step, 0)
     lax.fori_loop(0, 4, near_step, 0)
     lax.fori_loop(0, 4, last_step, 0)

time: 105 us -> 105 us (level)
  no operation moved by 1% of the time
where the time goes in v7:
time: 105 us; the launch traced here: 104 us
  Pallas kernels  103 us (98%)
  local copies, waits for them, and re-layouts  1.31 us (1%)
    pallas_call x1, Pallas kernels, per_device(): pl.pallas_call(kernel, out_shape=jax.ShapeDtypeStruct((4 * ZBLOCK, WIDE),...  103 us

profile of v7, /device:TPU:1, one launch (start us, length us, event | category | flops | bytes accessed | tf_op | source)
XLA Modules:
  0.0 104.4 jit_solution(3942235349601525532)
XLA Ops:
  0.0 103.1 %shard_map.46 = bf16[576,1792]{1,0:T(8,128)(2,1)S(1)} custom-call(s32[8]{0:T(128)} %count_hbm.1, s32[8]{0:T(128)} %owner_hbm.1, bf16[144,7168]{1,0:T(8,128)(2,1)} %bitcast.5, bf16[1792,1792]{1,0:T(8,128)(2,1)} %bitcast.4), custom_call_target="tpu_custom_call" | custom-call | flops 14797504512 | bytes 20000000 | tf_op jit(solution)/shard_map/pallas_call | solution.py:393
  103.1 1.3 %copy.6 = bf16[576,1,1792]{2,0,1:T(8,128)(2,1)} copy(bf16[576,1,1792]{2,0,1:T(8,128)(2,1)S(1)} %bitcast.3) | data formatting | bytes 4128768
